TPU v7x, 32 devices: a whole 2x2x4 slice. The times are simulated.
32 devices in a mesh: space: 8 (over z, x), kern: 4 (over y, core).
Axes of the slice: x: 2, y: 2, z: 4, core: 2. Of those that a mesh axis runs over, the one named last changes fastest.
Arguments:
- mask: bfloat16 [4096, 4096], P('space'), may hold values from -1 to 1
- kernels: float32 [2, 16, 512, 512], P(None, 'kern', 'space'), may hold values from -4 to 4
- target: int32 [1024, 1024], P('space'), may hold values 0 or 1
Outputs:
- gradient: float32 [4096, 4096], P('space')
- resist: float32 [1024, 1024], P('space')
All inputs are finite; a program needn't handle non-finite values. No bound on the sum of `target` on one device may be relied on, other than what follows from the above.
Results may differ from a plain program's by a relative error of at most 0.0003.
Values sent between devices are 32-bit elements; how exact they have to be, the bound alone decides.
A program may use at most 64 MiB of HBM per device.

v0:
```python
import jax
import jax.numpy as jnp
from jax import lax
from jax.sharding import PartitionSpec as P

N = 4096
B = 512
G = 1024
steepness = 8.0
threshold = 1.5
highest = lax.Precision.HIGHEST
block_limit = 1024


def phases(left, right, modulus):
    product = left[:, None] * right[None, :] % modulus
    return product.astype(jnp.float32) * (2.0 * jnp.pi / modulus)


def column_table(pixels, frequency, length):
    angle = phases(pixels, frequency, length)
    return jnp.concatenate([jnp.cos(angle), -jnp.sin(angle)], axis=1)


def row_table(pixels, frequency, length):
    angle = phases(pixels, frequency, length)
    return jnp.concatenate([jnp.cos(angle), -jnp.sin(angle)], axis=1) / length


def grid_table(frequency, points):
    angle = phases(frequency, jnp.arange(points, dtype=jnp.int32), points)
    return jnp.concatenate([jnp.cos(angle), jnp.sin(angle)], axis=1)


def forward_columns(mask, frequency):
    rows = mask.shape[0]
    span = min(block_limit, N)
    count = frequency.shape[0]

    def step(index, running):
        start = index * span
        table = column_table(start + jnp.arange(span, dtype=jnp.int32), frequency, N)
        piece = lax.dynamic_slice_in_dim(mask, start, span, 1).astype(jnp.float32)
        return running + lax.dot_general(table, piece, (((0,), (1,)), ((), ())), precision=highest)

    running = lax.fori_loop(0, N // span, step, jnp.zeros((2 * count, rows), jnp.float32))
    return running.reshape(2, count, rows)


def forward_rows(arrived):
    count = arrived.shape[1]
    flat = arrived.reshape(2 * count, N)
    frequency = jnp.arange(B, dtype=jnp.int32) - B // 2
    span = min(block_limit, N)

    def step(index, running):
        start = index * span
        table = row_table(start + jnp.arange(span, dtype=jnp.int32), frequency, N)
        piece = lax.dynamic_slice_in_dim(flat, start, span, 1)
        return running + jnp.dot(piece, table, precision=highest)

    running = lax.fori_loop(0, N // span, step, jnp.zeros((2 * count, 2 * B), jnp.float32))
    real_part = running[:count, :B] - running[count:, B:]
    imag_part = running[:count, B:] + running[count:, :B]
    return jnp.stack([real_part, imag_part])


def adjoint_rows(sum_re, sum_im):
    count = sum_re.shape[0]
    stacked = jnp.concatenate(
        [jnp.concatenate([sum_re, sum_im], axis=1), jnp.concatenate([sum_im, -sum_re], axis=1)],
        axis=0,
    )
    frequency = jnp.arange(B, dtype=jnp.int32) - B // 2
    span = min(block_limit, N)

    def step(index, output):
        start = index * span
        table = row_table(start + jnp.arange(span, dtype=jnp.int32), frequency, N)
        piece = lax.dot_general(stacked, table, (((1,), (1,)), ((), ())), precision=highest)
        return lax.dynamic_update_slice_in_dim(output, piece, start, 1)

    output = lax.fori_loop(0, N // span, step, jnp.zeros((2 * count, N), jnp.float32))
    return output.reshape(2, count, N)


def add_columns(total, spectrum, frequency):
    span = min(block_limit, N)

    def step(index, running):
        start = index * span
        table = column_table(start + jnp.arange(span, dtype=jnp.int32), frequency, N)
        piece = lax.dot_general(spectrum, table, (((0,), (1,)), ((), ())), precision=highest)
        current = lax.dynamic_slice_in_dim(running, start, span, 1)
        return lax.dynamic_update_slice_in_dim(running, current + piece, start, 1)

    return lax.fori_loop(0, N // span, step, total)


def local(mask, kernels, target):
    rows = mask.shape[0]
    kern_count = lax.axis_size("kern")
    space_count = lax.axis_size("space")
    group = lax.axis_index("kern")
    per_space = B // space_count
    per_group = per_space // kern_count
    frequency = jnp.arange(B, dtype=jnp.int32) - B // 2
    subset = (
        per_space * jnp.arange(space_count, dtype=jnp.int32)[:, None]
        + per_group * group
        + jnp.arange(per_group, dtype=jnp.int32)[None, :]
    )
    columns = forward_columns(mask, subset.reshape(-1) - B // 2)
    arrived = lax.all_to_all(columns, "space", split_axis=1, concat_axis=2, tiled=True)
    spectrum = lax.all_gather(forward_rows(arrived), "kern", axis=1, tiled=True)
    kern_swap = jnp.swapaxes(kernels, 1, 2)
    kernel_count = kern_swap.shape[2]
    spec_re = spectrum[0][:, None, :]
    spec_im = spectrum[1][:, None, :]
    prod_re = kern_swap[0] * spec_re - kern_swap[1] * spec_im
    prod_im = kern_swap[0] * spec_im + kern_swap[1] * spec_re
    grid = grid_table(frequency, G)
    lifted = jnp.dot(
        jnp.stack([prod_re, prod_im]).reshape(2 * per_space * kernel_count, B),
        grid,
        precision=highest,
    )
    lifted = lifted.reshape(2, per_space, kernel_count, 2 * G)
    coarse_re = lifted[0, :, :, :G] - lifted[1, :, :, G:]
    coarse_im = lifted[0, :, :, G:] + lifted[1, :, :, :G]
    coarse = jnp.stack([coarse_re, coarse_im], axis=1)
    gathered = lax.all_to_all(coarse, "space", split_axis=3, concat_axis=0, tiled=True)
    grid_rows = gathered.shape[3]
    image = lax.dot_general(
        gathered.reshape(B, 2 * kernel_count * grid_rows),
        grid,
        (((0,), (0,)), ((), ())),
        precision=highest,
    )
    image = image.reshape(2, kernel_count, grid_rows, 2 * G)
    field_re = image[0, :, :, :G] - image[1, :, :, G:]
    field_im = image[0, :, :, G:] + image[1, :, :, :G]
    partial_light = jnp.sum(field_re * field_re + field_im * field_im, axis=0) / (B * B)
    intensity = lax.psum(partial_light, "kern")
    resist = jax.nn.sigmoid(steepness * (intensity - threshold))
    slope = 2.0 * (resist - target.astype(jnp.float32)) * steepness * resist * (1.0 - resist)
    scale = 2.0 * slope / (B * B)
    grad_re = scale * field_re
    grad_im = scale * field_im
    mixed = jnp.stack(
        [
            jnp.concatenate([grad_re, grad_im], axis=-1),
            jnp.concatenate([grad_im, -grad_re], axis=-1),
        ]
    )
    mixed = mixed.reshape(2 * kernel_count * grid_rows, 2 * G)
    backward = lax.dot_general(grid, mixed, (((1,), (1,)), ((), ())), precision=highest)
    backward = backward.reshape(B, 2, kernel_count, grid_rows)
    returned = lax.all_to_all(backward, "space", split_axis=0, concat_axis=3, tiled=True)
    back_re = returned[:, 0]
    back_im = returned[:, 1]
    mixed_two = jnp.stack(
        [
            jnp.concatenate([back_re, back_im], axis=-1),
            jnp.concatenate([back_im, -back_re], axis=-1),
        ]
    )
    mixed_two = mixed_two.reshape(2 * per_space * kernel_count, 2 * G)
    spectral = lax.dot_general(mixed_two, grid, (((1,), (1,)), ((), ())), precision=highest)
    spectral = spectral.reshape(2, per_space, kernel_count, B)
    sum_re = jnp.sum(kern_swap[0] * spectral[0] + kern_swap[1] * spectral[1], axis=1)
    sum_im = jnp.sum(kern_swap[0] * spectral[1] - kern_swap[1] * spectral[0], axis=1)
    empty = jnp.zeros((rows, N), jnp.float32)
    shares = (
        lax.psum_scatter(sum_re, "kern", scatter_dimension=0, tiled=True),
        lax.psum_scatter(sum_im, "kern", scatter_dimension=0, tiled=True),
    )
    delta = adjoint_rows(shares[0], shares[1])
    landed = lax.all_to_all(delta, "space", split_axis=2, concat_axis=1, tiled=True)
    ordering = (
        per_group * jnp.arange(kern_count, dtype=jnp.int32)[:, None, None]
        + per_space * jnp.arange(space_count, dtype=jnp.int32)[None, :, None]
        + jnp.arange(per_group, dtype=jnp.int32)[None, None, :]
    )
    ordered_freq = ordering.reshape(-1) - B // 2
    piece = lax.all_gather(landed, "kern", axis=1, tiled=True)
    width = piece.shape[1]
    gradient = add_columns(empty, piece.reshape(2 * width, rows), ordered_freq)
    return (gradient, resist)


def solution(mesh):
    in_specs = (P("space", None), P(None, "kern", "space", None), P("space", None))
    out_specs = (P("space", None), P("space", None))
    return jax.shard_map(local, mesh=mesh, in_specs=in_specs, out_specs=out_specs, check_vma=False)
```

profile of v0, /device:TPU:0, one launch (start us, length us, event | category | flops | bytes accessed | tf_op | source)
XLA Modules:
  0.0 641.8 jit_solution(11022036640361063977)
XLA Ops:
  7.2 22.0 %while.66 = (s32[]{:T(128)}, f32[256,512]{1,0:T(8,128)S(1)}, bf16[512,4096]{1,0:T(8,128)(2,1)}, s32[8]{0:T(128)S(1)}, s32[]{:T(128)}, /*index=5*/s32[]{:T(128)}, s32[]{:T(128)}, s32[]{:T(128)}) while((s32[]{:T(128)}, f32[256,512]{1,0:T(8,128)S(1)}, bf16[512,4096]{1,0:T(8,128)(2,1)}, s32[8]{0:T(128)S(1)}, s32[]{:T(128)}, ...), condition=%wide.region_1.2_spmd.clone, body=%wide.region_0.1_spmd.clone.sunk | while | flops 1613104384 | bytes 4204733 | solution.py:46
  30.4 7.3 %all-to-all-start = ((f32[2,128,512]{2,0,1:T(2,128)}), f32[2,128,512]{2,0,1:T(2,128)S(1)}, u32[]{:S(2)}, u32[]{:S(2)}) async-start(f32[2,128,512]{2,0,1:T(2,128)} %copy.57), calls=%async_computation | async-start | bytes 1048576 | tf_op jit(solution)/shard_map/all_to_all | solution.py:114
  37.7 9.6 %fusion.78 = (f32[512,1024]{1,0:T(8,128)S(1)}, f32[512,1024]{1,0:T(8,128)}) fusion(s32[512]{0:T(512)S(1)} %iota_add_fusion.6), kind=kLoop, calls=%fused_computation.130 | loop fusion | flops 7340032 | bytes 4196352 | tf_op jit(solution)/shard_map/cos | solution.py:32
  47.3 4.8 all-to-all-done
  53.6 47.6 %while.67 = (s32[]{:T(128)}, f32[32,1024]{1,0:T(8,128)S(1)}, f32[32,4096]{1,0:T(8,128)}, s32[]{:T(128)}, s32[]{:T(128)}, /*index=5*/s32[]{:T(128)}, s32[]{:T(128)}) while((s32[]{:T(128)}, f32[32,1024]{1,0:T(8,128)S(1)}, f32[32,4096]{1,0:T(8,128)}, s32[]{:T(128)}, s32[]{:T(128)}, /*index=5*/s32[]{:T(128)}, s32[]{:T(128)}) %tuple.199), condition=%wide.region_3.4_spmd.clone, body=%wide.region_2.3_spmd.clone.sunk | while | flops 412681728 | bytes 8794261 | solution.py:62
  53.9 8.3 %fusion.116 = (f32[1024,512]{1,0:T(8,128)S(1)}, f32[1024,512]{1,0:T(8,128)S(1)}) fusion(s32[512]{0:T(512)S(1)} %iota_add_fusion.17, s32[1024]{0:T(1024)S(1)} %iota_add_fusion.18), kind=kLoop, calls=%fused_computation.79.clone.1 | loop fusion | flops 7864320 | bytes 4200448 | tf_op jit(solution)/shard_map/while/body/eval_jaxpr/cos | solution.py:27
  65.7 8.3 %fusion.116 = (f32[1024,512]{1,0:T(8,128)S(1)}, f32[1024,512]{1,0:T(8,128)S(1)}) fusion(s32[512]{0:T(512)S(1)} %iota_add_fusion.17, s32[1024]{0:T(1024)S(1)} %iota_add_fusion.18), kind=kLoop, calls=%fused_computation.79.clone.1 | loop fusion | flops 7864320 | bytes 4200448 | tf_op jit(solution)/shard_map/while/body/eval_jaxpr/cos | solution.py:27
  77.6 8.3 %fusion.116 = (f32[1024,512]{1,0:T(8,128)S(1)}, f32[1024,512]{1,0:T(8,128)S(1)}) fusion(s32[512]{0:T(512)S(1)} %iota_add_fusion.17, s32[1024]{0:T(1024)S(1)} %iota_add_fusion.18), kind=kLoop, calls=%fused_computation.79.clone.1 | loop fusion | flops 7864320 | bytes 4200448 | tf_op jit(solution)/shard_map/while/body/eval_jaxpr/cos | solution.py:27
  89.4 8.3 %fusion.116 = (f32[1024,512]{1,0:T(8,128)S(1)}, f32[1024,512]{1,0:T(8,128)S(1)}) fusion(s32[512]{0:T(512)S(1)} %iota_add_fusion.17, s32[1024]{0:T(1024)S(1)} %iota_add_fusion.18), kind=kLoop, calls=%fused_computation.79.clone.1 | loop fusion | flops 7864320 | bytes 4200448 | tf_op jit(solution)/shard_map/while/body/eval_jaxpr/cos | solution.py:27
  101.3 6.2 all_gather.6
  107.7 6.9 %fusion.61 = f32[2,64,4,2048]{3,1,2,0:T(8,128)S(1)} fusion(f32[512,1024]{1,0:T(8,128)S(1)} %copy-done.2, f32[512,1024]{1,0:T(8,128)S(1)} %get-tuple-element.572, f32[1,64,4,512]{3,1,2,0:T(8,128)S(1)} %get-tuple-element.563, f32[1,64,4,512]{3,1,2,0:T(8,128)S(1)} %get-tuple-element.562), kind=kOutput, calls=%fused_computation.97 | convolution fusion | flops 6443761664 | bytes 9437184 | tf_op jit(solution)/shard_map/dot_general | solution.py:123
  116.4 4.8 copy.60
  121.2 7.8 %reshape.172 = f32[8,1,65536]{2,1,0:T(1,128)} reshape(f32[1024,2,4,64]{3,2,1,0:T(4,128)} %bitcast.117) | data formatting | bytes 4194304
  129.0 53.8 %all_to_all.66 = f32[8,1,65536]{2,1,0:T(1,128)} all-to-all(f32[8,1,65536]{2,1,0:T(1,128)} %reshape.172), channel_id=1, replica_groups=mesh['space'=8,'kern'=4] {'space'}, dimensions={0} | all-to-all | bytes 4194304 | tf_op jit(solution)/shard_map/all_to_all | solution.py:132
  183.3 8.5 %reduce = f32[8,65536]{1,0:T(8,128)} reduce(f32[8,1,65536]{2,1,0:T(1,128)} %all_to_all.66, f32[]{:T(128)} %broadcast.375), dimensions={1}, to_apply=%all_to_all.51.reduce_sub_computation | reduce | bytes 4194308 | tf_op jit(solution)/shard_map/all_to_all | solution.py:132
  191.9 6.5 %reshape.173 = f32[1024,2,4,64]{3,2,1,0:T(4,128)} reshape(f32[8,65536]{1,0:T(8,128)} %reduce) | data formatting | bytes 4194304
  198.3 4.8 copy.61
  209.2 16.7 %fusion.59 = f32[2,4,128,2048]{3,2,1,0:T(8,128)S(1)} fusion(f32[2,4,128,512]{3,2,1,0:T(8,128)} %bitcast.122, f32[512,1024]{1,0:T(8,128)} %get-tuple-element.573, f32[512,1024]{1,0:T(8,128)S(1)} %get-tuple-element.572), kind=kOutput, calls=%fused_computation.95 | convolution fusion | flops 12885950464 | bytes 14680064 | tf_op jit(solution)/shard_map/dot_general | solution.py:134
  230.2 32.4 %all-reduce.2.cloned.1.call-done = f32[128,1024]{1,0:T(8,128)} async-done(((f32[128,1024]{1,0:T(8,128)}), f32[128,1024]{1,0:T(8,128)}) %all-reduce.2.cloned.1.call-update) | async-done | bytes 524304 | tf_op jit(solution)/shard_map/psum | solution.py:144
  264.8 4.5 fusion.88
  273.3 15.5 %fusion.54 = f32[512,2,4,128]{3,0,2,1:T(8,128)S(1)} fusion(f32[1,4,128,2048]{3,2,1,0:T(8,128)} %get-tuple-element.561, f32[1,4,128,2048]{3,2,1,0:T(8,128)} %get-tuple-element.560, f32[512,1024]{1,0:T(8,128)S(1)} %copy-done.3, f32[512,1024]{1,0:T(8,128)S(1)} %get-tuple-element.572), kind=kOutput, calls=%fused_computation.86 | convolution fusion | flops 12888047616 | bytes 14680064 | tf_op jit(solution)/shard_map/dot_general | solution.py:157
  290.1 53.1 %all_to_all.67 = f32[512,2,4,128]{3,2,1,0:T(4,128)S(1)} all-to-all(f32[512,2,4,128]{3,2,1,0:T(4,128)S(1)} %copy.63), channel_id=1, replica_groups=mesh['space'=8,'kern'=4] {'space'}, dimensions={0} | all-to-all | bytes 4194304 | tf_op jit(solution)/shard_map/all_to_all | solution.py:159
  351.5 4.7 copy.65
  356.2 5.3 reshape.168
  361.6 8.9 %fusion.71 = f32[512,512]{1,0:T(8,128)S(1)} fusion(f32[512,2048]{1,0:T(8,128)} %reshape.168, f32[512,1024]{1,0:T(8,128)} %get-tuple-element.573, f32[512,1024]{1,0:T(8,128)S(1)} %get-tuple-element.572), kind=kOutput, calls=%fused_computation.117 | convolution fusion | flops 6443499520 | bytes 9437184 | tf_op jit(solution)/shard_map/dot_general | solution.py:169
  372.8 17.0 %reduce-scatter.3.cloned.1.call-done = f32[16,512]{1,0:T(8,128)} async-done(((f32[64,512]{1,0:T(8,128)}), f32[16,512]{1,0:T(8,128)}) %reduce-scatter.3.cloned.1.call-update) | async-done | bytes 32784 | tf_op jit(solution)/shard_map/reduce_scatter | solution.py:175
  390.5 21.9 %reduce-scatter.5.cloned.1.call-done = f32[16,512]{1,0:T(8,128)} async-done(((f32[64,512]{1,0:T(8,128)}), f32[16,512]{1,0:T(8,128)}) %reduce-scatter.5.cloned.1.call-update) | async-done | bytes 32784 | tf_op jit(solution)/shard_map/reduce_scatter | solution.py:176
  413.3 49.2 %while.64 = (s32[]{:T(128)}, f32[32,4096]{1,0:T(8,128)S(1)}, f32[32,1024]{1,0:T(8,128)S(1)}, s32[]{:T(128)}, s32[]{:T(128)}, /*index=5*/s32[]{:T(128)}, s32[]{:T(128)}) while((s32[]{:T(128)}, f32[32,4096]{1,0:T(8,128)S(1)}, f32[32,1024]{1,0:T(8,128)S(1)}, s32[]{:T(128)}, s32[]{:T(128)}, /*index=5*/s32[]{:T(128)}, ...), condition=%wide.region_11.12_spmd.clone, body=%wide.region_10.11_spmd.clone.sunk | while | flops 412616192 | bytes 8663171 | solution.py:83
  413.5 8.3 %fusion.107 = (f32[1024,512]{1,0:T(8,128)S(1)}, f32[1024,512]{1,0:T(8,128)S(1)}) fusion(s32[512]{0:T(512)S(1)} %iota_add_fusion.13, s32[1024]{0:T(1024)S(1)} %iota_add_fusion.14), kind=kLoop, calls=%fused_computation.20.clone.1 | loop fusion | flops 7864320 | bytes 4200448 | tf_op jit(solution)/shard_map/while/body/eval_jaxpr/cos | solution.py:27
  425.8 8.3 %fusion.107 = (f32[1024,512]{1,0:T(8,128)S(1)}, f32[1024,512]{1,0:T(8,128)S(1)}) fusion(s32[512]{0:T(512)S(1)} %iota_add_fusion.13, s32[1024]{0:T(1024)S(1)} %iota_add_fusion.14), kind=kLoop, calls=%fused_computation.20.clone.1 | loop fusion | flops 7864320 | bytes 4200448 | tf_op jit(solution)/shard_map/while/body/eval_jaxpr/cos | solution.py:27
  438.0 8.3 %fusion.107 = (f32[1024,512]{1,0:T(8,128)S(1)}, f32[1024,512]{1,0:T(8,128)S(1)}) fusion(s32[512]{0:T(512)S(1)} %iota_add_fusion.13, s32[1024]{0:T(1024)S(1)} %iota_add_fusion.14), kind=kLoop, calls=%fused_computation.20.clone.1 | loop fusion | flops 7864320 | bytes 4200448 | tf_op jit(solution)/shard_map/while/body/eval_jaxpr/cos | solution.py:27
  450.3 8.3 %fusion.107 = (f32[1024,512]{1,0:T(8,128)S(1)}, f32[1024,512]{1,0:T(8,128)S(1)}) fusion(s32[512]{0:T(512)S(1)} %iota_add_fusion.13, s32[1024]{0:T(1024)S(1)} %iota_add_fusion.14), kind=kLoop, calls=%fused_computation.20.clone.1 | loop fusion | flops 7864320 | bytes 4200448 | tf_op jit(solution)/shard_map/while/body/eval_jaxpr/cos | solution.py:27
  462.5 4.3 copy.70
  466.8 7.4 %reshape.174 = f32[8,1,16384]{2,1,0:T(1,128)S(1)} reshape(f32[4096,2,16]{2,1,0:T(2,128)} %bitcast.119) | data formatting | bytes 1048576
  474.2 19.3 %all_to_all.68 = f32[8,1,16384]{2,1,0:T(1,128)S(1)} all-to-all(f32[8,1,16384]{2,1,0:T(1,128)S(1)} %reshape.174), channel_id=1, replica_groups=mesh['space'=8,'kern'=4] {'space'}, dimensions={0} | all-to-all | bytes 1048576 | tf_op jit(solution)/shard_map/all_to_all | solution.py:179
  495.4 7.6 %reshape.175 = f32[4096,2,16]{2,1,0:T(2,128)} reshape(f32[8,16384]{1,0:T(8,128)S(1)} %reduce.1) | data formatting | bytes 1048576
  503.0 6.3 copy.76
  509.4 20.8 %all-gather.2.cloned.1.call-done = f32[2,512,512]{2,1,0:T(8,128)} async-done(((f32[2,128,512]{2,1,0:T(8,128)}), f32[2,512,512]{2,1,0:T(8,128)}) %all-gather.2.cloned.1.call-update) | async-done | bytes 2097168 | tf_op jit(solution)/shard_map/all_gather | solution.py:186
  530.2 4.4 broadcast_in_dim.45.clone
  534.6 100.2 %while.65 = (s32[]{:T(128)}, f32[512,4096]{1,0:T(8,128)}, f32[1024,512]{1,0:T(8,128)}, s32[4,8]{1,0:T(4,128)S(1)}, s32[]{:T(128)}, /*index=5*/s32[]{:T(128)}, s32[]{:T(128)}, s32[]{:T(128)}) while((s32[]{:T(128)}, f32[512,4096]{1,0:T(8,128)}, f32[1024,512]{1,0:T(8,128)}, s32[4,8]{1,0:T(4,128)S(1)}, s32[]{:T(128)}, ...), condition=%wide.region_13.14_spmd.clone, body=%wide.region_12.13_spmd.clone.sunk | while | flops 6451890176 | bytes 39862572 | solution.py:97
  540.2 8.3 %fusion.111 = (f32[1024,512]{1,0:T(8,128)S(1)}, f32[1024,512]{1,0:T(8,128)S(1)}) fusion(s32[512]{0:T(512)S(1)} %sub.133, s32[1024]{0:T(1024)S(1)} %iota_add_fusion.15), kind=kLoop, calls=%fused_computation.39.clone.1 | loop fusion | flops 7864320 | bytes 4200448 | tf_op jit(solution)/shard_map/while/body/eval_jaxpr/cos | solution.py:22
  548.5 8.0 %bitcast_add_fusion.2 = f32[512,1024]{0,1:T(8,128)} fusion(f32[512,1024]{0,1:T(8,128)S(1)} %copy.92, f32[1024,512]{1,0:T(8,128)S(1)} %copy-done.1, f32[1024,512]{1,0:T(8,128)S(1)} %get-tuple-element.665, f32[1024,512]{1,0:T(8,128)S(1)} %get-tuple-element.666), kind=kOutput, calls=%fused_computation.37.clone.1 | convolution fusion | flops 6444023808 | bytes 10485760 | tf_op jit(solution)/shard_map/while/body/eval_jaxpr/dot_general | solution.py:93
  565.1 8.3 %fusion.111 = (f32[1024,512]{1,0:T(8,128)S(1)}, f32[1024,512]{1,0:T(8,128)S(1)}) fusion(s32[512]{0:T(512)S(1)} %sub.133, s32[1024]{0:T(1024)S(1)} %iota_add_fusion.15), kind=kLoop, calls=%fused_computation.39.clone.1 | loop fusion | flops 7864320 | bytes 4200448 | tf_op jit(solution)/shard_map/while/body/eval_jaxpr/cos | solution.py:22
  573.4 8.0 %bitcast_add_fusion.2 = f32[512,1024]{0,1:T(8,128)} fusion(f32[512,1024]{0,1:T(8,128)S(1)} %copy.92, f32[1024,512]{1,0:T(8,128)S(1)} %copy-done.1, f32[1024,512]{1,0:T(8,128)S(1)} %get-tuple-element.665, f32[1024,512]{1,0:T(8,128)S(1)} %get-tuple-element.666), kind=kOutput, calls=%fused_computation.37.clone.1 | convolution fusion | flops 6444023808 | bytes 10485760 | tf_op jit(solution)/shard_map/while/body/eval_jaxpr/dot_general | solution.py:93
  590.1 8.3 %fusion.111 = (f32[1024,512]{1,0:T(8,128)S(1)}, f32[1024,512]{1,0:T(8,128)S(1)}) fusion(s32[512]{0:T(512)S(1)} %sub.133, s32[1024]{0:T(1024)S(1)} %iota_add_fusion.15), kind=kLoop, calls=%fused_computation.39.clone.1 | loop fusion | flops 7864320 | bytes 4200448 | tf_op jit(solution)/shard_map/while/body/eval_jaxpr/cos | solution.py:22
  598.4 8.0 %bitcast_add_fusion.2 = f32[512,1024]{0,1:T(8,128)} fusion(f32[512,1024]{0,1:T(8,128)S(1)} %copy.92, f32[1024,512]{1,0:T(8,128)S(1)} %copy-done.1, f32[1024,512]{1,0:T(8,128)S(1)} %get-tuple-element.665, f32[1024,512]{1,0:T(8,128)S(1)} %get-tuple-element.666), kind=kOutput, calls=%fused_computation.37.clone.1 | convolution fusion | flops 6444023808 | bytes 10485760 | tf_op jit(solution)/shard_map/while/body/eval_jaxpr/dot_general | solution.py:93
  615.1 8.3 %fusion.111 = (f32[1024,512]{1,0:T(8,128)S(1)}, f32[1024,512]{1,0:T(8,128)S(1)}) fusion(s32[512]{0:T(512)S(1)} %sub.133, s32[1024]{0:T(1024)S(1)} %iota_add_fusion.15), kind=kLoop, calls=%fused_computation.39.clone.1 | loop fusion | flops 7864320 | bytes 4200448 | tf_op jit(solution)/shard_map/while/body/eval_jaxpr/cos | solution.py:22
  623.4 8.0 %bitcast_add_fusion.2 = f32[512,1024]{0,1:T(8,128)} fusion(f32[512,1024]{0,1:T(8,128)S(1)} %copy.92, f32[1024,512]{1,0:T(8,128)S(1)} %copy-done.1, f32[1024,512]{1,0:T(8,128)S(1)} %get-tuple-element.665, f32[1024,512]{1,0:T(8,128)S(1)} %get-tuple-element.666), kind=kOutput, calls=%fused_computation.37.clone.1 | convolution fusion | flops 6444023808 | bytes 10485760 | tf_op jit(solution)/shard_map/while/body/eval_jaxpr/dot_general | solution.py:93
  (137 shorter events, 123.4 us)
Async XLA Ops:
  30.4 21.7 %all-to-all-start = ((f32[2,128,512]{2,0,1:T(2,128)}), f32[2,128,512]{2,0,1:T(2,128)S(1)}, u32[]{:S(2)}, u32[]{:S(2)}) async-start(f32[2,128,512]{2,0,1:T(2,128)} %copy.57), calls=%async_computation | async-start | bytes 1048576 | tf_op jit(solution)/shard_map/all_to_all | solution.py:114
  37.6 225.0 %all-reduce.2.cloned.1.call-start = ((), (), s32[]{:S(2)}) async-start(), calls=%async_computation.6 | async-start | bytes 1048576 | tf_op jit(solution)/shard_map/psum | solution.py:144
  53.6 53.8 %copy-start.5 = (f32[2,4,64,512]{3,2,1,0:T(8,128)S(1)}, f32[2,4,64,512]{3,2,1,0:T(8,128)}, u32[]{:S(2)}) copy-start(f32[2,4,64,512]{3,2,1,0:T(8,128)} %param.12) | copy-start | bytes 3145732
  101.2 6.5 %copy-start.2 = (f32[512,1024]{1,0:T(8,128)S(1)}, f32[512,1024]{1,0:T(8,128)}, u32[]{:S(2)}) copy-start(f32[512,1024]{1,0:T(8,128)} %get-tuple-element.573) | copy-start | bytes 6291460
  225.9 3.4 copy-start
  230.2 159.6 %reduce-scatter.3.cloned.1.call-start = ((), (), s32[]{:S(2)}) async-start(), calls=%async_computation.7 | async-start | bytes 163840 | tf_op jit(solution)/shard_map/reduce_scatter | solution.py:175
  269.3 4.0 copy-start.3
  348.5 1.9 copy-start.4
  372.0 40.5 %reduce-scatter.5.cloned.1.call-start = ((), (), s32[]{:S(2)}) async-start(), calls=%async_computation.8 | async-start | bytes 163840 | tf_op jit(solution)/shard_map/reduce_scatter | solution.py:176
  372.7 157.5 %all-gather.2.cloned.1.call-start = ((), (), s32[]{:S(2)}) async-start(), calls=%async_computation.9 | async-start | bytes 2621440 | tf_op jit(solution)/shard_map/all_gather | solution.py:186
  540.1 8.3 %copy-start.1 = (f32[1024,512]{1,0:T(8,128)S(1)}, f32[1024,512]{1,0:T(8,128)}, u32[]{:S(2)}) copy-start(f32[1024,512]{1,0:T(8,128)} %get-tuple-element.762) | copy-start | bytes 6291460 | tf_op jit(solution)/shard_map/while
  565.1 8.3 %copy-start.1 = (f32[1024,512]{1,0:T(8,128)S(1)}, f32[1024,512]{1,0:T(8,128)}, u32[]{:S(2)}) copy-start(f32[1024,512]{1,0:T(8,128)} %get-tuple-element.762) | copy-start | bytes 6291460 | tf_op jit(solution)/shard_map/while
  590.1 8.3 %copy-start.1 = (f32[1024,512]{1,0:T(8,128)S(1)}, f32[1024,512]{1,0:T(8,128)}, u32[]{:S(2)}) copy-start(f32[1024,512]{1,0:T(8,128)} %get-tuple-element.762) | copy-start | bytes 6291460 | tf_op jit(solution)/shard_map/while
  615.1 8.3 %copy-start.1 = (f32[1024,512]{1,0:T(8,128)S(1)}, f32[1024,512]{1,0:T(8,128)}, u32[]{:S(2)}) copy-start(f32[1024,512]{1,0:T(8,128)} %get-tuple-element.762) | copy-start | bytes 6291460 | tf_op jit(solution)/shard_map/while
Sparse Core Ops, SparseCore 0:
  230.3 32.2 all-reduce.1
  372.1 17.5 reduce-scatter.2
  392.9 19.5 reduce-scatter.4
  509.4 20.7 all-gather.1
where the time goes:
time: 649 us; the launch traced here: 642 us
  other arithmetic  149 us (23%)
  blocking collectives  132 us (20%)
  matrix products  122 us (19%)
  local copies, waits for them, and re-layouts  118 us (18%)
  waiting for transfers between devices  97.6 us (15%)
  between operations  14.5 us (2%)
  starting transfers between devices  7.41 us (1%)
    cos x8, other arithmetic, row_table(): return jnp.concatenate([jnp.cos(angle), -jnp.sin(angle)], axis=1) / length  66.3 us
    all_to_all x1, blocking collectives, local(): lax.all_to_all(coarse, 'space', split_axis=3, concat_axis=0, tiled=True)  53.8 us
    all_to_all x1, blocking collectives, local(): lax.all_to_all(backward, 'space', split_axis=0, concat_axis=3, tiled=True)  53.1 us
    cos x8, other arithmetic, column_table(): return jnp.concatenate([jnp.cos(angle), -jnp.sin(angle)], axis=1)  41.7 us
    unnamed x15, local copies, waits for them, and re-layouts  33.1 us
    psum x1, waiting for transfers between devices, local(): intensity = lax.psum(partial_light, 'kern')  32.4 us
    dot_general x4, matrix products, step(): lax.dot_general(spectrum, table, (((0,), (1,)), ((), ())), precision=high...  32.1 us
    reduce_scatter x1, waiting for transfers between devices, local(): lax.psum_scatter(sum_im, 'kern', scatter_dimension=0, tiled=True)  21.9 us
  transfers between devices with their start and end apart: 5, of which 5 were waited for; matrix products, arithmetic and copies ran while one was open for 2% of the time, Pallas kernels for 0%

commit v1 on v0

--- a/solution.py
+++ b/solution.py
@@ -129,7 +129,19 @@
     coarse_re = lifted[0, :, :, :G] - lifted[1, :, :, G:]
     coarse_im = lifted[0, :, :, G:] + lifted[1, :, :, :G]
     coarse = jnp.stack([coarse_re, coarse_im], axis=1)
-    gathered = lax.all_to_all(coarse, "space", split_axis=3, concat_axis=0, tiled=True)
+    ways, here = (lax.axis_size("space"), lax.axis_index("space"))
+    width_2 = coarse.shape[3] // ways
+    lengths = list(coarse.shape)
+    lengths[3] = width_2
+    height = lengths[0]
+    lengths[0] = height * ways
+    full = jnp.zeros(lengths, coarse.dtype)
+    for mask_2 in range(ways):
+        part = lax.dynamic_slice_in_dim(coarse, (here ^ mask_2) * width_2, width_2, axis=3)
+        if mask_2:
+            part = lax.ppermute(part, "space", [(d, d ^ mask_2) for d in range(ways)])
+        full = lax.dynamic_update_slice_in_dim(full, part, (here ^ mask_2) * height, axis=0)
+    gathered = full
     grid_rows = gathered.shape[3]
     image = lax.dot_general(
         gathered.reshape(B, 2 * kernel_count * grid_rows),

time: 649 us -> 618 us (0.952)
  blocking collectives: 132 us -> 78.7 us
  starting transfers between devices: 7.41 us -> 17.8 us
  waiting for transfers between devices: 97.6 us -> 107 us
  local copies, waits for them, and re-layouts: 118 us -> 127 us
  other arithmetic: 149 us -> 141 us
    all_to_all x1 -> x0, blocking collectives: 53.8 us -> none  [local(): lax.all_to_all(coarse, 'space', split_axis=3, concat_axis=0, tiled=True)]
    dynamic_update_slice x0 -> x8, local copies, waits for them, and re-layouts: none -> 29.8 us  [local(): lax.dynamic_update_slice_in_dim(full, part, (here ^ mask_2) * height, axi...]
    unnamed x15 -> x19, local copies, waits for them, and re-layouts: 33.1 us -> 20.6 us
    ppermute x0 -> x7, starting transfers between devices: none -> 10.4 us  [local(): part = lax.ppermute(part, 'space', [(d, d ^ mask_2) for d in range(ways)])]
    ppermute x0 -> x7, waiting for transfers between devices: none -> 9 us  [local(): part = lax.ppermute(part, 'space', [(d, d ^ mask_2) for d in range(ways)])]
    all_to_all x1 -> x0, other arithmetic: 8.52 us -> none  [local(): lax.all_to_all(coarse, 'space', split_axis=3, concat_axis=0, tiled=True)]
  transfers between devices with their start and end apart: 5 -> 12, of which waited for: 5 -> 6; matrix products, arithmetic and copies ran while one was open for 2% -> 8% of each run, Pallas kernels for 0% -> 0%
where the time goes in v1:
time: 618 us; the launch traced here: 611 us
  other arithmetic  141 us (23%)
  local copies, waits for them, and re-layouts  127 us (21%)
  matrix products  122 us (20%)
  waiting for transfers between devices  107 us (17%)
  blocking collectives  78.7 us (13%)
  starting transfers between devices  17.8 us (3%)
  between operations  14.7 us (2%)
    cos x8, other arithmetic, row_table(): return jnp.concatenate([jnp.cos(angle), -jnp.sin(angle)], axis=1) / length  66.3 us
    all_to_all x1, blocking collectives, local(): lax.all_to_all(backward, 'space', split_axis=0, concat_axis=3, tiled=True)  53.1 us
    cos x8, other arithmetic, column_table(): return jnp.concatenate([jnp.cos(angle), -jnp.sin(angle)], axis=1)  41.7 us
    psum x1, waiting for transfers between devices, local(): intensity = lax.psum(partial_light, 'kern')  33.1 us
    dot_general x4, matrix products, step(): lax.dot_general(spectrum, table, (((0,), (1,)), ((), ())), precision=high...  32 us
    dynamic_update_slice x8, local copies, waits for them, and re-layouts, local(): lax.dynamic_update_slice_in_dim(full, part, (here ^ mask_2) * height, axi...  29.8 us
    reduce_scatter x1, waiting for transfers between devices, local(): lax.psum_scatter(sum_im, 'kern', scatter_dimension=0, tiled=True)  22 us
    all_gather x1, waiting for transfers between devices, local(): piece = lax.all_gather(landed, 'kern', axis=1, tiled=True)  20.8 us
  transfers between devices with their start and end apart: 12, of which 6 were waited for; matrix products, arithmetic and copies ran while one was open for 8% of the time, Pallas kernels for 0%

profile of v1, /device:TPU:0, one launch (start us, length us, event | category | flops | bytes accessed | tf_op | source)
XLA Modules:
  0.0 610.6 jit_solution(11609482439682798718)
XLA Ops:
  7.2 22.0 %while.66 = (s32[]{:T(128)}, f32[256,512]{1,0:T(8,128)S(1)}, bf16[512,4096]{1,0:T(8,128)(2,1)}, s32[8]{0:T(128)S(1)}, s32[]{:T(128)}, /*index=5*/s32[]{:T(128)}, s32[]{:T(128)}, s32[]{:T(128)}) while((s32[]{:T(128)}, f32[256,512]{1,0:T(8,128)S(1)}, bf16[512,4096]{1,0:T(8,128)(2,1)}, s32[8]{0:T(128)S(1)}, s32[]{:T(128)}, ...), condition=%wide.region_1.2_spmd.clone, body=%wide.region_0.1_spmd.clone.sunk | while | flops 1613104384 | bytes 4204733 | solution.py:46
  30.4 7.3 %all-to-all-start = ((f32[2,128,512]{2,0,1:T(2,128)}), f32[2,128,512]{2,0,1:T(2,128)S(1)}, u32[]{:S(2)}, u32[]{:S(2)}) async-start(f32[2,128,512]{2,0,1:T(2,128)} %copy.79), calls=%async_computation | async-start | bytes 1048576 | tf_op jit(solution)/shard_map/all_to_all | solution.py:114
  37.7 9.6 %fusion.79 = (f32[512,1024]{1,0:T(8,128)S(1)}, f32[512,1024]{1,0:T(8,128)}) fusion(s32[512]{0:T(512)S(1)} %iota_add_fusion.6), kind=kLoop, calls=%fused_computation.146 | loop fusion | flops 7340032 | bytes 4196352 | tf_op jit(solution)/shard_map/cos | solution.py:32
  47.3 4.8 all-to-all-done
  53.6 47.6 %while.67 = (s32[]{:T(128)}, f32[32,1024]{1,0:T(8,128)S(1)}, f32[32,4096]{1,0:T(8,128)}, s32[]{:T(128)}, s32[]{:T(128)}, /*index=5*/s32[]{:T(128)}, s32[]{:T(128)}) while((s32[]{:T(128)}, f32[32,1024]{1,0:T(8,128)S(1)}, f32[32,4096]{1,0:T(8,128)}, s32[]{:T(128)}, s32[]{:T(128)}, /*index=5*/s32[]{:T(128)}, s32[]{:T(128)}) %tuple.205), condition=%wide.region_3.4_spmd.clone, body=%wide.region_2.3_spmd.clone.sunk | while | flops 412681728 | bytes 8794261 | solution.py:62
  53.9 8.3 %fusion.124 = (f32[1024,512]{1,0:T(8,128)S(1)}, f32[1024,512]{1,0:T(8,128)S(1)}) fusion(s32[512]{0:T(512)S(1)} %iota_add_fusion.17, s32[1024]{0:T(1024)S(1)} %iota_add_fusion.18), kind=kLoop, calls=%fused_computation.79.clone.1 | loop fusion | flops 7864320 | bytes 4200448 | tf_op jit(solution)/shard_map/while/body/eval_jaxpr/cos | solution.py:27
  65.7 8.3 %fusion.124 = (f32[1024,512]{1,0:T(8,128)S(1)}, f32[1024,512]{1,0:T(8,128)S(1)}) fusion(s32[512]{0:T(512)S(1)} %iota_add_fusion.17, s32[1024]{0:T(1024)S(1)} %iota_add_fusion.18), kind=kLoop, calls=%fused_computation.79.clone.1 | loop fusion | flops 7864320 | bytes 4200448 | tf_op jit(solution)/shard_map/while/body/eval_jaxpr/cos | solution.py:27
  77.6 8.3 %fusion.124 = (f32[1024,512]{1,0:T(8,128)S(1)}, f32[1024,512]{1,0:T(8,128)S(1)}) fusion(s32[512]{0:T(512)S(1)} %iota_add_fusion.17, s32[1024]{0:T(1024)S(1)} %iota_add_fusion.18), kind=kLoop, calls=%fused_computation.79.clone.1 | loop fusion | flops 7864320 | bytes 4200448 | tf_op jit(solution)/shard_map/while/body/eval_jaxpr/cos | solution.py:27
  89.4 8.3 %fusion.124 = (f32[1024,512]{1,0:T(8,128)S(1)}, f32[1024,512]{1,0:T(8,128)S(1)}) fusion(s32[512]{0:T(512)S(1)} %iota_add_fusion.17, s32[1024]{0:T(1024)S(1)} %iota_add_fusion.18), kind=kLoop, calls=%fused_computation.79.clone.1 | loop fusion | flops 7864320 | bytes 4200448 | tf_op jit(solution)/shard_map/while/body/eval_jaxpr/cos | solution.py:27
  101.3 6.3 %all_gather.6 = f32[2,64,512]{2,1,0:T(8,128)S(1)} all-gather(f32[2,16,512]{2,1,0:T(8,128)S(1)} %pad_maximum_fusion.6), channel_id=1, replica_groups=mesh['space'=8,'kern'=4] {'kern'}, dimensions={1}, use_global_device_ids=true | all-gather | bytes 327680 | tf_op jit(solution)/shard_map/all_gather | solution.py:115
  107.8 6.8 %fusion.61 = f32[2,64,4,2048]{3,1,2,0:T(8,128)S(1)} fusion(f32[512,1024]{1,0:T(8,128)S(1)} %copy-done.2, f32[512,1024]{1,0:T(8,128)S(1)} %get-tuple-element.580, f32[1,64,4,512]{3,1,2,0:T(8,128)S(1)} %get-tuple-element.571, f32[1,64,4,512]{3,1,2,0:T(8,128)S(1)} %get-tuple-element.570), kind=kOutput, calls=%fused_computation.113 | convolution fusion | flops 6443761664 | bytes 9437184 | tf_op jit(solution)/shard_map/dot_general | solution.py:123
  127.8 9.0 %collective-permute-done.1 = f32[64,2,4,128]{3,0,2,1:T(8,128)} collective-permute-done((f32[64,2,4,128]{3,0,2,1:T(8,128)}, f32[64,2,4,128]{3,0,2,1:T(8,128)}, u32[]{:S(2)}, u32[]{:S(2)}) %collective-permute-start.1) | collective-permute-done | bytes 262176 | tf_op jit(solution)/shard_map/ppermute | solution.py:142
  144.8 4.3 dynamic_update_slice.45
  154.9 4.3 dynamic_update_slice.47
  164.9 4.3 dynamic_update_slice.49
  176.3 16.7 %fusion.59 = f32[2,4,128,2048]{3,2,1,0:T(8,128)S(1)} fusion(f32[512,2,4,128]{0,3,2,1:T(8,128)} %dynamic_update_slice.51, f32[512,1024]{1,0:T(8,128)} %get-tuple-element.581, f32[512,1024]{1,0:T(8,128)S(1)} %get-tuple-element.580), kind=kOutput, calls=%fused_computation.111 | convolution fusion | flops 12885950464 | bytes 14680064 | tf_op jit(solution)/shard_map/dot_general | solution.py:146
  197.3 33.1 %all-reduce.2.cloned.1.call-done = f32[128,1024]{1,0:T(8,128)} async-done(((f32[128,1024]{1,0:T(8,128)}), f32[128,1024]{1,0:T(8,128)}) %all-reduce.2.cloned.1.call-update) | async-done | bytes 524304 | tf_op jit(solution)/shard_map/psum | solution.py:156
  232.4 4.5 fusion.97
  237.0 3.9 maximum_bitcast_fusion
  240.9 15.5 %fusion.54 = f32[512,2,4,128]{3,0,2,1:T(8,128)S(1)} fusion(f32[1,4,128,2048]{3,2,1,0:T(8,128)} %get-tuple-element.561, f32[1,4,128,2048]{3,2,1,0:T(8,128)} %get-tuple-element.560, f32[512,1024]{1,0:T(8,128)S(1)} %copy-done.3, f32[512,1024]{1,0:T(8,128)S(1)} %get-tuple-element.580), kind=kOutput, calls=%fused_computation.86 | convolution fusion | flops 12888047616 | bytes 14680064 | tf_op jit(solution)/shard_map/dot_general | solution.py:169
  257.7 53.1 %all_to_all.51 = f32[512,2,4,128]{3,2,1,0:T(4,128)S(1)} all-to-all(f32[512,2,4,128]{3,2,1,0:T(4,128)S(1)} %copy.90), channel_id=1, replica_groups=mesh['space'=8,'kern'=4] {'space'}, dimensions={0} | all-to-all | bytes 4194304 | tf_op jit(solution)/shard_map/all_to_all | solution.py:171
  319.1 4.7 copy.92
  323.9 5.3 reshape.167
  329.1 8.9 %fusion.72 = f32[512,512]{1,0:T(8,128)S(1)} fusion(f32[512,2048]{1,0:T(8,128)} %reshape.167, f32[512,1024]{1,0:T(8,128)} %get-tuple-element.581, f32[512,1024]{1,0:T(8,128)S(1)} %get-tuple-element.580), kind=kOutput, calls=%fused_computation.133 | convolution fusion | flops 6443499520 | bytes 9437184 | tf_op jit(solution)/shard_map/dot_general | solution.py:181
  341.2 17.0 %reduce-scatter.3.cloned.1.call-done = f32[16,512]{1,0:T(8,128)} async-done(((f32[64,512]{1,0:T(8,128)}), f32[16,512]{1,0:T(8,128)}) %reduce-scatter.3.cloned.1.call-update) | async-done | bytes 32784 | tf_op jit(solution)/shard_map/reduce_scatter | solution.py:187
  358.9 22.0 %reduce-scatter.5.cloned.1.call-done = f32[16,512]{1,0:T(8,128)} async-done(((f32[64,512]{1,0:T(8,128)}), f32[16,512]{1,0:T(8,128)}) %reduce-scatter.5.cloned.1.call-update) | async-done | bytes 32784 | tf_op jit(solution)/shard_map/reduce_scatter | solution.py:188
  381.8 49.2 %while.64 = (s32[]{:T(128)}, f32[32,4096]{1,0:T(8,128)S(1)}, f32[32,1024]{1,0:T(8,128)S(1)}, s32[]{:T(128)}, s32[]{:T(128)}, /*index=5*/s32[]{:T(128)}, s32[]{:T(128)}) while((s32[]{:T(128)}, f32[32,4096]{1,0:T(8,128)S(1)}, f32[32,1024]{1,0:T(8,128)S(1)}, s32[]{:T(128)}, s32[]{:T(128)}, /*index=5*/s32[]{:T(128)}, ...), condition=%wide.region_11.12_spmd.clone, body=%wide.region_10.11_spmd.clone.sunk | while | flops 412616192 | bytes 8663171 | solution.py:83
  382.0 8.3 %fusion.115 = (f32[1024,512]{1,0:T(8,128)S(1)}, f32[1024,512]{1,0:T(8,128)S(1)}) fusion(s32[512]{0:T(512)S(1)} %iota_add_fusion.13, s32[1024]{0:T(1024)S(1)} %iota_add_fusion.14), kind=kLoop, calls=%fused_computation.20.clone.1 | loop fusion | flops 7864320 | bytes 4200448 | tf_op jit(solution)/shard_map/while/body/eval_jaxpr/cos | solution.py:27
  390.3 3.9 fusion.116
  394.2 8.3 %fusion.115 = (f32[1024,512]{1,0:T(8,128)S(1)}, f32[1024,512]{1,0:T(8,128)S(1)}) fusion(s32[512]{0:T(512)S(1)} %iota_add_fusion.13, s32[1024]{0:T(1024)S(1)} %iota_add_fusion.14), kind=kLoop, calls=%fused_computation.20.clone.1 | loop fusion | flops 7864320 | bytes 4200448 | tf_op jit(solution)/shard_map/while/body/eval_jaxpr/cos | solution.py:27
  406.5 8.3 %fusion.115 = (f32[1024,512]{1,0:T(8,128)S(1)}, f32[1024,512]{1,0:T(8,128)S(1)}) fusion(s32[512]{0:T(512)S(1)} %iota_add_fusion.13, s32[1024]{0:T(1024)S(1)} %iota_add_fusion.14), kind=kLoop, calls=%fused_computation.20.clone.1 | loop fusion | flops 7864320 | bytes 4200448 | tf_op jit(solution)/shard_map/while/body/eval_jaxpr/cos | solution.py:27
  418.7 8.3 %fusion.115 = (f32[1024,512]{1,0:T(8,128)S(1)}, f32[1024,512]{1,0:T(8,128)S(1)}) fusion(s32[512]{0:T(512)S(1)} %iota_add_fusion.13, s32[1024]{0:T(1024)S(1)} %iota_add_fusion.14), kind=kLoop, calls=%fused_computation.20.clone.1 | loop fusion | flops 7864320 | bytes 4200448 | tf_op jit(solution)/shard_map/while/body/eval_jaxpr/cos | solution.py:27
  430.9 4.3 copy.97
  435.3 7.4 %reshape.171 = f32[8,1,16384]{2,1,0:T(1,128)S(1)} reshape(f32[4096,2,16]{2,1,0:T(2,128)} %bitcast.117) | data formatting | bytes 1048576
  442.7 19.3 %all_to_all.52 = f32[8,1,16384]{2,1,0:T(1,128)S(1)} all-to-all(f32[8,1,16384]{2,1,0:T(1,128)S(1)} %reshape.171), channel_id=1, replica_groups=mesh['space'=8,'kern'=4] {'space'}, dimensions={0} | all-to-all | bytes 1048576 | tf_op jit(solution)/shard_map/all_to_all | solution.py:191
  464.4 7.6 %reshape.172 = f32[4096,2,16]{2,1,0:T(2,128)} reshape(f32[8,16384]{1,0:T(8,128)S(1)} %reduce) | data formatting | bytes 1048576
  472.0 6.2 %copy.103 = f32[2,16,8,512]{3,1,2,0:T(8,128)} copy(f32[2,16,8,512]{1,0,3,2:T(2,128)} %bitcast.118) | data formatting | bytes 1048576 | tf_op jit(solution)/shard_map/all_to_all | solution.py:191
  478.4 20.8 %all-gather.2.cloned.1.call-done = f32[2,512,512]{2,1,0:T(8,128)} async-done(((f32[2,128,512]{2,1,0:T(8,128)}), f32[2,512,512]{2,1,0:T(8,128)}) %all-gather.2.cloned.1.call-update) | async-done | bytes 2097168 | tf_op jit(solution)/shard_map/all_gather | solution.py:198
  499.1 4.4 broadcast_in_dim.48.clone
  503.6 100.0 %while.65 = (s32[]{:T(128)}, f32[512,4096]{1,0:T(8,128)}, f32[1024,512]{1,0:T(8,128)}, s32[4,8]{1,0:T(4,128)S(1)}, s32[]{:T(128)}, /*index=5*/s32[]{:T(128)}, s32[]{:T(128)}, s32[]{:T(128)}) while((s32[]{:T(128)}, f32[512,4096]{1,0:T(8,128)}, f32[1024,512]{1,0:T(8,128)}, s32[4,8]{1,0:T(4,128)S(1)}, s32[]{:T(128)}, ...), condition=%wide.region_13.14_spmd.clone, body=%wide.region_12.13_spmd.clone.sunk | while | flops 6451890176 | bytes 39862572 | solution.py:97
  509.1 8.3 %fusion.119 = (f32[1024,512]{1,0:T(8,128)S(1)}, f32[1024,512]{1,0:T(8,128)S(1)}) fusion(s32[512]{0:T(512)S(1)} %sub.133, s32[1024]{0:T(1024)S(1)} %iota_add_fusion.15), kind=kLoop, calls=%fused_computation.39.clone.1 | loop fusion | flops 7864320 | bytes 4200448 | tf_op jit(solution)/shard_map/while/body/eval_jaxpr/cos | solution.py:22
  517.4 8.0 %bitcast_add_fusion.2 = f32[512,1024]{0,1:T(8,128)} fusion(f32[512,1024]{0,1:T(8,128)S(1)} %copy.119, f32[1024,512]{1,0:T(8,128)S(1)} %copy-done.1, f32[1024,512]{1,0:T(8,128)S(1)} %get-tuple-element.673, f32[1024,512]{1,0:T(8,128)S(1)} %get-tuple-element.674), kind=kOutput, calls=%fused_computation.37.clone.1 | convolution fusion | flops 6444023808 | bytes 10485760 | tf_op jit(solution)/shard_map/while/body/eval_jaxpr/dot_general | solution.py:93
  534.0 8.3 %fusion.119 = (f32[1024,512]{1,0:T(8,128)S(1)}, f32[1024,512]{1,0:T(8,128)S(1)}) fusion(s32[512]{0:T(512)S(1)} %sub.133, s32[1024]{0:T(1024)S(1)} %iota_add_fusion.15), kind=kLoop, calls=%fused_computation.39.clone.1 | loop fusion | flops 7864320 | bytes 4200448 | tf_op jit(solution)/shard_map/while/body/eval_jaxpr/cos | solution.py:22
  542.3 8.0 %bitcast_add_fusion.2 = f32[512,1024]{0,1:T(8,128)} fusion(f32[512,1024]{0,1:T(8,128)S(1)} %copy.119, f32[1024,512]{1,0:T(8,128)S(1)} %copy-done.1, f32[1024,512]{1,0:T(8,128)S(1)} %get-tuple-element.673, f32[1024,512]{1,0:T(8,128)S(1)} %get-tuple-element.674), kind=kOutput, calls=%fused_computation.37.clone.1 | convolution fusion | flops 6444023808 | bytes 10485760 | tf_op jit(solution)/shard_map/while/body/eval_jaxpr/dot_general | solution.py:93
  559.0 8.3 %fusion.119 = (f32[1024,512]{1,0:T(8,128)S(1)}, f32[1024,512]{1,0:T(8,128)S(1)}) fusion(s32[512]{0:T(512)S(1)} %sub.133, s32[1024]{0:T(1024)S(1)} %iota_add_fusion.15), kind=kLoop, calls=%fused_computation.39.clone.1 | loop fusion | flops 7864320 | bytes 4200448 | tf_op jit(solution)/shard_map/while/body/eval_jaxpr/cos | solution.py:22
  567.3 8.0 %bitcast_add_fusion.2 = f32[512,1024]{0,1:T(8,128)} fusion(f32[512,1024]{0,1:T(8,128)S(1)} %copy.119, f32[1024,512]{1,0:T(8,128)S(1)} %copy-done.1, f32[1024,512]{1,0:T(8,128)S(1)} %get-tuple-element.673, f32[1024,512]{1,0:T(8,128)S(1)} %get-tuple-element.674), kind=kOutput, calls=%fused_computation.37.clone.1 | convolution fusion | flops 6444023808 | bytes 10485760 | tf_op jit(solution)/shard_map/while/body/eval_jaxpr/dot_general | solution.py:93
  583.9 8.3 %fusion.119 = (f32[1024,512]{1,0:T(8,128)S(1)}, f32[1024,512]{1,0:T(8,128)S(1)}) fusion(s32[512]{0:T(512)S(1)} %sub.133, s32[1024]{0:T(1024)S(1)} %iota_add_fusion.15), kind=kLoop, calls=%fused_computation.39.clone.1 | loop fusion | flops 7864320 | bytes 4200448 | tf_op jit(solution)/shard_map/while/body/eval_jaxpr/cos | solution.py:22
  592.2 8.0 %bitcast_add_fusion.2 = f32[512,1024]{0,1:T(8,128)} fusion(f32[512,1024]{0,1:T(8,128)S(1)} %copy.119, f32[1024,512]{1,0:T(8,128)S(1)} %copy-done.1, f32[1024,512]{1,0:T(8,128)S(1)} %get-tuple-element.673, f32[1024,512]{1,0:T(8,128)S(1)} %get-tuple-element.674), kind=kOutput, calls=%fused_computation.37.clone.1 | convolution fusion | flops 6444023808 | bytes 10485760 | tf_op jit(solution)/shard_map/while/body/eval_jaxpr/dot_general | solution.py:93
  (167 shorter events, 147.9 us)
Async XLA Ops:
  30.4 21.7 %all-to-all-start = ((f32[2,128,512]{2,0,1:T(2,128)}), f32[2,128,512]{2,0,1:T(2,128)S(1)}, u32[]{:S(2)}, u32[]{:S(2)}) async-start(f32[2,128,512]{2,0,1:T(2,128)} %copy.79), calls=%async_computation | async-start | bytes 1048576 | tf_op jit(solution)/shard_map/all_to_all | solution.py:114
  37.6 192.7 %all-reduce.2.cloned.1.call-start = ((), (), s32[]{:S(2)}) async-start(), calls=%async_computation.5 | async-start | bytes 1048576 | tf_op jit(solution)/shard_map/psum | solution.py:156
  53.6 54.0 %copy-start.6 = (f32[2,4,64,512]{3,2,1,0:T(8,128)S(1)}, f32[2,4,64,512]{3,2,1,0:T(8,128)}, u32[]{:S(2)}) copy-start(f32[2,4,64,512]{3,2,1,0:T(8,128)} %param.12) | copy-start | bytes 3145732
  101.2 6.6 %copy-start.2 = (f32[512,1024]{1,0:T(8,128)S(1)}, f32[512,1024]{1,0:T(8,128)}, u32[]{:S(2)}) copy-start(f32[512,1024]{1,0:T(8,128)} %get-tuple-element.581) | copy-start | bytes 6291460
  115.2 1.0 copy-start.5
  117.2 9.1 %collective-permute-start = (f32[64,2,4,128]{3,0,2,1:T(8,128)}, f32[64,2,4,128]{3,0,2,1:T(8,128)}, u32[]{:S(2)}, u32[]{:S(2)}) collective-permute-start(f32[64,2,4,128]{3,0,2,1:T(8,128)} %get-tuple-element.564), channel_id=1, source_target_pairs={{0,4},{4,0},{8,12},{12,8},{16,20},{20,16},{24,28},{28,24},{1,5},{5... | collective-permute-start | bytes 786440 | tf_op jit(solution)/shard_map/ppermute | solution.py:142
  118.7 18.1 %collective-permute-start.1 = (f32[64,2,4,128]{3,0,2,1:T(8,128)}, f32[64,2,4,128]{3,0,2,1:T(8,128)}, u32[]{:S(2)}, u32[]{:S(2)}) collective-permute-start(f32[64,2,4,128]{3,0,2,1:T(8,128)} %get-tuple-element.565), channel_id=1, source_target_pairs={{0,8},{4,12},{8,0},{12,4},{16,24},{20,28},{24,16},{28,20},{1,9},{5... | collective-permute-start | bytes 786440 | tf_op jit(solution)/shard_map/ppermute | solution.py:142
  118.7 35.0 %collective-permute-start.2 = (f32[64,2,4,128]{3,0,2,1:T(8,128)}, f32[64,2,4,128]{3,0,2,1:T(8,128)}, u32[]{:S(2)}, u32[]{:S(2)}) collective-permute-start(f32[64,2,4,128]{3,0,2,1:T(8,128)} %get-tuple-element.566), channel_id=1, source_target_pairs={{0,12},{4,8},{8,4},{12,0},{16,28},{20,24},{24,20},{28,16},{1,13},{... | collective-permute-start | bytes 786440 | tf_op jit(solution)/shard_map/ppermute | solution.py:142
  120.7 38.5 %collective-permute-start.3 = (f32[64,2,4,128]{3,0,2,1:T(8,128)}, f32[64,2,4,128]{3,0,2,1:T(8,128)}, u32[]{:S(2)}, u32[]{:S(2)}) collective-permute-start(f32[64,2,4,128]{3,0,2,1:T(8,128)} %get-tuple-element.567), channel_id=1, source_target_pairs={{0,16},{4,20},{8,24},{12,28},{16,0},{20,4},{24,8},{28,12},{1,17},{... | collective-permute-start | bytes 786440 | tf_op jit(solution)/shard_map/ppermute | solution.py:142
  122.7 41.1 %collective-permute-start.4 = (f32[64,2,4,128]{3,0,2,1:T(8,128)}, f32[64,2,4,128]{3,0,2,1:T(8,128)}, u32[]{:S(2)}, u32[]{:S(2)}) collective-permute-start(f32[64,2,4,128]{3,0,2,1:T(8,128)} %get-tuple-element.569), channel_id=1, source_target_pairs={{0,20},{4,16},{8,28},{12,24},{16,4},{20,0},{24,12},{28,8},{1,21},{... | collective-permute-start | bytes 786440 | tf_op jit(solution)/shard_map/ppermute | solution.py:142
  126.4 42.8 %collective-permute-start.5 = (f32[64,2,4,128]{3,0,2,1:T(8,128)}, f32[64,2,4,128]{3,0,2,1:T(8,128)S(1)}, u32[]{:S(2)}, u32[]{:S(2)}) collective-permute-start(f32[64,2,4,128]{3,0,2,1:T(8,128)} %get-tuple-element.568), channel_id=1, source_target_pairs={{0,24},{4,28},{8,16},{12,20},{16,8},{20,12},{24,0},{28,4},{1,25},{... | collective-permute-start | bytes 786440 | tf_op jit(solution)/shard_map/ppermute | solution.py:142
  136.8 35.5 %collective-permute-start.6 = (f32[64,2,4,128]{3,0,2,1:T(8,128)}, f32[64,2,4,128]{3,0,2,1:T(8,128)S(1)}, u32[]{:S(2)}, u32[]{:S(2)}) collective-permute-start(f32[64,2,4,128]{3,0,2,1:T(8,128)} %get-tuple-element.562), channel_id=1, source_target_pairs={{0,28},{4,24},{8,20},{12,16},{16,12},{20,8},{24,4},{28,0},{1,29},{... | collective-permute-start | bytes 786440 | tf_op jit(solution)/shard_map/ppermute | solution.py:142
  193.0 3.4 copy-start
  193.0 37.4 %copy-start.8 = (s32[128,1024]{1,0:T(8,128)S(1)}, s32[128,1024]{1,0:T(8,128)}, u32[]{:S(2)}) copy-start(s32[128,1024]{1,0:T(8,128)} %param.13) | copy-start | bytes 1572868
  197.2 160.9 %reduce-scatter.3.cloned.1.call-start = ((), (), s32[]{:S(2)}) async-start(), calls=%async_computation.6 | async-start | bytes 163840 | tf_op jit(solution)/shard_map/reduce_scatter | solution.py:187
  236.9 4.0 copy-start.3
  316.1 1.9 copy-start.4
  338.0 1.2 copy-start.7
  340.4 40.5 %reduce-scatter.5.cloned.1.call-start = ((), (), s32[]{:S(2)}) async-start(), calls=%async_computation.7 | async-start | bytes 163840 | tf_op jit(solution)/shard_map/reduce_scatter | solution.py:188
  341.1 158.0 %all-gather.2.cloned.1.call-start = ((), (), s32[]{:S(2)}) async-start(), calls=%async_computation.8 | async-start | bytes 2621440 | tf_op jit(solution)/shard_map/all_gather | solution.py:198
  509.1 8.3 %copy-start.1 = (f32[1024,512]{1,0:T(8,128)S(1)}, f32[1024,512]{1,0:T(8,128)}, u32[]{:S(2)}) copy-start(f32[1024,512]{1,0:T(8,128)} %get-tuple-element.770) | copy-start | bytes 6291460 | tf_op jit(solution)/shard_map/while
  534.0 8.3 %copy-start.1 = (f32[1024,512]{1,0:T(8,128)S(1)}, f32[1024,512]{1,0:T(8,128)}, u32[]{:S(2)}) copy-start(f32[1024,512]{1,0:T(8,128)} %get-tuple-element.770) | copy-start | bytes 6291460 | tf_op jit(solution)/shard_map/while
  558.9 8.3 %copy-start.1 = (f32[1024,512]{1,0:T(8,128)S(1)}, f32[1024,512]{1,0:T(8,128)}, u32[]{:S(2)}) copy-start(f32[1024,512]{1,0:T(8,128)} %get-tuple-element.770) | copy-start | bytes 6291460 | tf_op jit(solution)/shard_map/while
  583.9 8.3 %copy-start.1 = (f32[1024,512]{1,0:T(8,128)S(1)}, f32[1024,512]{1,0:T(8,128)}, u32[]{:S(2)}) copy-start(f32[1024,512]{1,0:T(8,128)} %get-tuple-element.770) | copy-start | bytes 6291460 | tf_op jit(solution)/shard_map/while
Sparse Core Ops, SparseCore 0:
  197.4 32.9 all-reduce.1
  340.5 17.5 reduce-scatter.2
  361.3 19.5 reduce-scatter.4
  478.4 20.7 all-gather.1
